TPU v7x, 32 devices: a whole 2x2x4 slice. The times are simulated.
32 devices in a mesh: img: 2 (over y), space: 16 (over z, x, core).
Axes of the slice: x: 2, y: 2, z: 4, core: 2. Of those that a mesh axis runs over, the one named last changes fastest.
Arguments:
- images: float32 [2, 384, 96, 128], P('img', 'space'), may hold values from -6 to 6
- pairings: int32 [3, 2], replicated, may hold values from 0 to 1, as said below
Outputs:
- advected: float32 [2, 384, 96, 128], P('img', 'space')
- velocity: float32 [2, 3, 384, 96, 128], P('img', None, 'space')
Inputs may be any that keep to these rules, and one draw needn't show every extreme that they name: Each row of pairings is a permutation of the 2 images; an image may be its own partner.
All inputs are finite; a program needn't handle non-finite values.
Results may differ from a plain program's by a relative error of at most 0.00018.
Values sent between devices are 32-bit elements; how exact they have to be, the bound alone decides.
No kernel may reach another device: no remote copies, remote signals or barrier semaphores. Data moves between devices by JAX's collectives and lax.ppermute only.
A program may use at most 64 MiB of HBM per device.

v0:
```python
import math

import jax
import jax.numpy as jnp
from jax import lax
from jax.sharding import PartitionSpec as P

RADIUS = 4
PAIRINGS = 3


gauss_sigma = 1.5
step_scale = 8.0
floor_product = 0.25
floor_variance = 0.5


def extended_2(value, sides, width):
    for axis, dim in sides:
        peers, length = (lax.axis_size(axis), value.shape[dim])
        up = [(i, (i + 1) % peers) for i in range(peers - 1)]
        down = [(j, i) for i, j in up]
        last = lax.slice_in_dim(value, length - width, length, axis=dim)
        initial = lax.slice_in_dim(value, 0, width, axis=dim)
        before = lax.ppermute(last, axis, up)
        after = lax.ppermute(initial, axis, down)
        value = jnp.concatenate([before, value, after], axis=dim)
    return value


def gauss_taps(radius):
    raw_taps = [
        math.exp(-(offset * offset) / (2.0 * gauss_sigma * gauss_sigma))
        for offset in range(-radius, radius + 1)
    ]
    total_weight = sum(raw_taps)
    return [raw_weight / total_weight for raw_weight in raw_taps]


def padded_along(volume, dimension, margin):
    widths = [(0, 0)] * volume.ndim
    widths[dimension] = (margin, margin)
    return jnp.pad(volume, widths)


def window(padded, dimension, offset, length):
    return lax.slice_in_dim(padded, offset, offset + length, axis=dimension)


def sum_three(volume, dimension):
    length = volume.shape[dimension]
    padded = padded_along(volume, dimension, 1)
    return (
        window(padded, dimension, 0, length)
        + window(padded, dimension, 1, length)
        + window(padded, dimension, 2, length)
    )


def sum_three_valid(volume, dimension):
    length = volume.shape[dimension] - 2
    return (
        window(volume, dimension, 0, length)
        + window(volume, dimension, 1, length)
        + window(volume, dimension, 2, length)
    )


def box_rows(extended):
    return sum_three(sum_three_valid(extended, 0), 1) / 9.0


def central(volume, dimension):
    length = volume.shape[dimension]
    padded = padded_along(volume, dimension, 1)
    return (window(padded, dimension, 2, length) - window(padded, dimension, 0, length)) * 0.5


def gradient_rows(extended):
    center = extended[1:-1]
    along_rows = (extended[2:] - extended[:-2]) * 0.5
    return jnp.stack([along_rows, central(center, 1), central(center, 2)])


def smooth_along(volume, dimension, weights):
    length = volume.shape[dimension]
    padded = padded_along(volume, dimension, len(weights) // 2)
    result = weights[0] * window(padded, dimension, 0, length)
    for tap_index in range(1, len(weights)):
        result = result + weights[tap_index] * window(padded, dimension, tap_index, length)
    return result


def smooth_rows(extended, weights):
    length = extended.shape[1] - len(weights) + 1
    result = weights[0] * window(extended, 1, 0, length)
    for tap_index in range(1, len(weights)):
        result = result + weights[tap_index] * window(extended, 1, tap_index, length)
    return result


def drive_total(own_extended, partner_extended):
    mean_own = box_rows(own_extended)
    spread_own = box_rows(own_extended * own_extended) - mean_own * mean_own
    center_own = own_extended[1:-1] - mean_own
    guarded_spread = jnp.maximum(spread_own, floor_variance)
    drive_sum = None
    for pairing_row in range(PAIRINGS):
        partner = partner_extended[pairing_row]
        mean_partner = box_rows(partner)
        cross_term = box_rows(own_extended * partner) - mean_own * mean_partner
        spread_partner = box_rows(partner * partner) - mean_partner * mean_partner
        factor = 2.0 * cross_term / jnp.maximum(spread_own * spread_partner, floor_product)
        ratio_term = cross_term / guarded_spread
        pair_term = factor * (partner[1:-1] - mean_partner - ratio_term * center_own)
        drive_sum = pair_term if drive_sum is None else drive_sum + pair_term
    return drive_sum


def advect_rows(near_own, velocity):
    center = near_own[1:-1]
    backward = center - near_own[:-2]
    forward = near_own[2:] - center
    change = jnp.maximum(velocity[0], 0.0) * backward + jnp.minimum(velocity[0], 0.0) * forward
    for dimension in range(1, 3):
        length = center.shape[dimension]
        padded = padded_along(center, dimension, 1)
        backward = center - window(padded, dimension, 0, length)
        forward = window(padded, dimension, 2, length) - center
        speed_part = velocity[dimension]
        change = change + (
            jnp.maximum(speed_part, 0.0) * backward + jnp.minimum(speed_part, 0.0) * forward
        )
    return center - change


def fetch_partners(stacked, pairings):
    image_rank = lax.axis_index("img")
    partner_ids = lax.dynamic_slice_in_dim(pairings, image_rank, 1, 1)[:, 0]
    piece_block = lax.all_gather(stacked, "img", axis=0, tiled=True)
    block_count = piece_block.shape[0]
    candidates = jnp.arange(block_count, dtype=jnp.int32)
    selector = (partner_ids[:, None] == candidates[None, :]).astype(jnp.float32)
    return jnp.einsum("kn,nryz->kryz", selector, piece_block, precision=lax.Precision.HIGHEST)


def shards(images, pairings):
    weights = gauss_taps(RADIUS)
    own_brick = images[0]
    near_own = extended_2(own_brick, (("space", 0),), 1)
    partners = fetch_partners(images, pairings)
    partner_extended = extended_2(partners, (("space", 1),), 1)
    drive_sum = drive_total(near_own, partner_extended)
    force = drive_sum[None] * gradient_rows(near_own)
    force_extended = extended_2(force, (("space", 1),), RADIUS)
    smoothed = smooth_rows(force_extended, weights)
    smoothed = smooth_along(smoothed, 2, weights)
    smoothed = smooth_along(smoothed, 3, weights)
    velocity = step_scale * smoothed
    advected = advect_rows(near_own, velocity)
    return (advected[None], velocity[None])


def solution(mesh):
    return jax.shard_map(
        shards,
        mesh=mesh,
        in_specs=(P("img", "space", None, None), P()),
        out_specs=(P("img", "space", None, None), P("img", None, "space", None, None)),
        check_vma=False,
    )
```

profile of v0, /device:TPU:9, one launch (start us, length us, event | category | flops | bytes accessed | tf_op | source)
XLA Modules:
  0.0 136.2 jit_solution(14987764733620427128)
XLA Ops:
  7.2 0.0 copy-start
  7.2 0.0 copy-start.2
  7.2 0.0 all-gather.2.cloned.1.call-start
  7.2 0.7 all-gather.2.cloned.1.call-update
  7.9 0.5 copy-done.2
  8.5 3.7 %collective-permute-start = (f32[1,96,128]{2,1,0:T(8,128)S(1)}, f32[1,96,128]{2,1,0:T(8,128)}, u32[]{:S(2)}, u32[]{:S(2)}) collective-permute-start(f32[1,96,128]{2,1,0:T(8,128)S(1)} %get-tuple-element.24), channel_id=1, source_target_pairs={{0,1},{1,2},{2,3},{3,4},{4,5},{5,6},{6,7},{7,8},{8,9},{9,10},{10,1... | collective-permute-start | bytes 147464 | tf_op jit(solution)/shard_map/ppermute | solution.py:25
  12.2 1.9 %collective-permute-start.1 = (f32[1,96,128]{2,1,0:T(8,128)S(1)}, f32[1,96,128]{2,1,0:T(8,128)}, u32[]{:S(2)}, u32[]{:S(2)}) collective-permute-start(f32[1,96,128]{2,1,0:T(8,128)S(1)} %get-tuple-element.25), channel_id=1, source_target_pairs={{1,0},{2,1},{3,2},{4,3},{5,4},{6,5},{7,6},{8,7},{9,8},{10,9},{11,1... | collective-permute-start | bytes 147464 | tf_op jit(solution)/shard_map/ppermute | solution.py:26
  14.1 0.0 copy-done
  14.1 32.7 %all-gather.2.cloned.1.call-done = f32[2,24,96,128]{3,2,1,0:T(8,128)} async-done(((f32[1,24,96,128]{3,2,1,0:T(8,128)}), f32[2,24,96,128]{3,2,1,0:T(8,128)}) %all-gather.2.cloned.1.call-update) | async-done | bytes 2359312 | tf_op jit(solution)/shard_map/all_gather | solution.py:140
  46.8 8.8 %fusion.44 = f32[3,24,96,128]{3,0,2,1:T(4,128)S(1)} fusion(f32[2,24,96,128]{3,2,1,0:T(8,128)} %all-gather.2.cloned.1.call-done, s32[3]{0:T(128)S(1)} %dynamic-slice_bitcast_fusion), kind=kOutput, calls=%fused_computation.73 | convolution fusion | flops 21233670 | bytes 5898252 | tf_op jit(solution)/shard_map/kn,nryz->kryz/dot_general | solution.py:144
  55.7 0.9 constant_dynamic-update-slice_fusion.6
  56.7 3.7 %collective-permute-start.2 = (f32[3,1,96,128]{3,2,1,0:T(8,128)S(1)}, f32[3,1,96,128]{3,2,1,0:T(8,128)S(1)}, u32[]{:S(2)}, u32[]{:S(2)}) collective-permute-start(f32[3,1,96,128]{3,2,1,0:T(8,128)S(1)} %get-tuple-element.18), channel_id=1, source_target_pairs={{0,1},{1,2},{2,3},{3,4},{4,5},{5,6},{6,7},{7,8},{8,9},{9,10},{10,1... | collective-permute-start | bytes 442376 | tf_op jit(solution)/shard_map/ppermute | solution.py:25
  60.3 0.0 collective-permute-done
  60.3 0.0 collective-permute-done.1
  60.3 2.8 %fusion.113 = (f32[24,96,128]{2,1,0:T(8,128)S(1)}, f32[1,24,96,128]{3,2,1,0:T(8,128)S(1)}, f32[1,24,96,128]{3,2,1,0:T(8,128)S(1)}, f32[1,24,96,128]{3,2,1,0:T(8,128)}) fusion(f32[1,96,128]{2,1,0:T(8,128)} %collective-permute-done.1, f32[24,96,128]{2,1,0:T(8,128)S(1)} %bitcast.108, f32[1,96,128]{2,1,0:T(8,128)} %collective-permute-done), kind=kLoop, calls=%fused_computation.191 | loop fusion | flops 2949120 | bytes 5996544 | tf_op jit(solution)/shard_map/add | solution.py:63
  63.2 1.2 slice.503
  64.4 2.1 %collective-permute-start.3 = (f32[3,1,96,128]{3,2,1,0:T(8,128)S(1)}, f32[3,1,96,128]{3,2,1,0:T(8,128)S(1)}, u32[]{:S(2)}, u32[]{:S(2)}) collective-permute-start(f32[3,1,96,128]{3,2,1,0:T(8,128)S(1)} %get-tuple-element.17), channel_id=1, source_target_pairs={{1,0},{2,1},{3,2},{4,3},{5,4},{6,5},{7,6},{8,7},{9,8},{10,9},{11,1... | collective-permute-start | bytes 442376 | tf_op jit(solution)/shard_map/ppermute | solution.py:26
  66.5 0.0 collective-permute-done.2
  66.6 0.7 constant_dynamic-update-slice_fusion.4
  67.2 2.5 %constant_dynamic-update-slice_fusion.3 = (f32[3,25,96,128]{3,2,1,0:T(8,128)}, f32[3,26,96,128]{3,2,1,0:T(8,128)S(1)}) fusion(f32[3,25,96,128]{3,2,1,0:T(8,128)} %get-tuple-element.26, f32[3,24,96,128]{3,2,1,0:T(8,128)S(1)} %get-tuple-element.3, f32[3,26,96,128]{3,2,1,0:T(8,128)S(1)} %get-tuple-element.27), kind=kLoop, calls=%fused_computation.224 | loop fusion | bytes 10616832 | tf_op jit(solution)/shard_map/concatenate | solution.py:27
  69.7 1.2 collective-permute-done.3
  70.9 1.8 %fusion.47 = (f32[26,96,128]{2,1,0:T(8,128)S(1)}, f32[26,96,128]{2,1,0:T(8,128)S(1)}, f32[26,96,128]{2,1,0:T(8,128)S(1)}, f32[26,96,128]{2,1,0:T(8,128)S(1)}, f3...) fusion(f32[3,26,96,128]{3,2,1,0:T(8,128)S(1)} %get-tuple-element.29, ...), kind=kLoop, calls=%fused_computation.104 | loop fusion | flops 2875392 | bytes 14057472 | tf_op jit(solution)/shard_map/mul | solution.py:111
  72.8 0.1 slice_add_fusion.12
  72.9 0.3 slice_add_fusion
  73.2 0.2 slice_add_fusion.4
  73.5 0.2 slice_add_fusion.8
  73.7 3.1 %fusion.110 = (f32[24,96,128]{2,1,0:T(8,128)S(1)}, f32[24,96,128]{2,1,0:T(8,128)S(1)}, f32[24,96,128]{2,1,0:T(8,128)S(1)}) fusion(f32[3,25,96,128]{3,2,1,0:T(8,128)S(1)} %get-tuple-element.28, f32[3,25,96,128]{3,2,1,0:T(8,128)} %get-tuple-element.15, f32[3,24,96,128]{3,2,1,0:T(8,128)S(1)} %get-tuple-element.3, f32[24,96,128]{2,1,0:T(8,128)S(1)} %bitcast.111), kind=kLoop, calls=%fused_computation.185 | loop fusion | flops 1769472 | bytes 14155776 | tf_op jit(solution)/shard_map/add | solution.py:63
  76.9 0.0 copy-start.3
  76.9 6.6 %fusion.75 = f32[24,96,128]{2,1,0:T(8,128)S(1)} fusion(f32[24,96,128]{2,1,0:T(8,128)S(1)} %get-tuple-element.34, f32[24,96,128]{2,1,0:T(8,128)S(1)} %get-tuple-element.32, f32[24,96,128]{2,1,0:T(8,128)S(1)} %get-tuple-element.30, f32[24,96,128]{2,1,0:T(8,128)S(1)} %bitcast.112, f32[24,96,128]{2,1,0:T(8,128)S(1)} %get-tuple-element.31, ...), kind=kLoop, calls=%fused_computation.132 | loop fusion | flops 23003136 | bytes 18874368 | tf_op jit(solution)/shard_map/add | solution.py:116
  83.5 0.0 copy-done.3
  83.5 0.4 maximum_multiply_fusion
  84.0 0.1 fusion.135
  84.1 2.5 %collective-permute-start.4 = (f32[3,4,96,128]{3,2,1,0:T(8,128)S(1)}, f32[3,4,96,128]{3,2,1,0:T(8,128)S(1)}, u32[]{:S(2)}, u32[]{:S(2)}) collective-permute-start(f32[3,4,96,128]{3,2,1,0:T(8,128)S(1)} %get-tuple-element.13), channel_id=1, source_target_pairs={{0,1},{1,2},{2,3},{3,4},{4,5},{5,6},{6,7},{7,8},{8,9},{9,10},{10,1... | collective-permute-start | bytes 1769480 | tf_op jit(solution)/shard_map/ppermute | solution.py:25
  86.5 2.1 %collective-permute-start.5 = (f32[3,4,96,128]{3,2,1,0:T(8,128)S(1)}, f32[3,4,96,128]{3,2,1,0:T(8,128)S(1)}, u32[]{:S(2)}, u32[]{:S(2)}) collective-permute-start(f32[3,4,96,128]{3,2,1,0:T(8,128)S(1)} %get-tuple-element.14), channel_id=1, source_target_pairs={{1,0},{2,1},{3,2},{4,3},{5,4},{6,5},{7,6},{8,7},{9,8},{10,9},{11,1... | collective-permute-start | bytes 1769480 | tf_op jit(solution)/shard_map/ppermute | solution.py:26
  88.7 11.0 %collective-permute-done.4 = f32[3,4,96,128]{3,2,1,0:T(8,128)S(1)} collective-permute-done((f32[3,4,96,128]{3,2,1,0:T(8,128)S(1)}, f32[3,4,96,128]{3,2,1,0:T(8,128)S(1)}, u32[]{:S(2)}, u32[]{:S(2)}) %collective-permute-start.4) | collective-permute-done | bytes 589856 | tf_op jit(solution)/shard_map/ppermute | solution.py:25
  99.7 2.5 %collective-permute-done.5 = f32[3,4,96,128]{3,2,1,0:T(8,128)S(1)} collective-permute-done((f32[3,4,96,128]{3,2,1,0:T(8,128)S(1)}, f32[3,4,96,128]{3,2,1,0:T(8,128)S(1)}, u32[]{:S(2)}, u32[]{:S(2)}) %collective-permute-start.5) | collective-permute-done | bytes 589856 | tf_op jit(solution)/shard_map/ppermute | solution.py:26
  102.2 4.1 %fusion.3 = f32[3,24,96,128]{3,2,1,0:T(8,128)S(1)} fusion(f32[3,24,96,128]{3,2,1,0:T(8,128)S(1)} %maximum_multiply_fusion, f32[3,4,96,128]{3,2,1,0:T(8,128)S(1)} %collective-permute-done.5, f32[3,4,96,128]{3,2,1,0:T(8,128)S(1)} %collective-permute-done.4), kind=kLoop, calls=%fused_computation.23 | loop fusion | flops 22118400 | bytes 8257536 | tf_op jit(solution)/shard_map/add | solution.py:98
  106.2 3.8 %multiply_add_fusion = f32[3,24,96,128]{3,2,1,0:T(8,128)S(1)} fusion(f32[3,24,96,128]{3,2,1,0:T(8,128)S(1)} %fusion.3), kind=kLoop, calls=%fused_computation.62 | loop fusion | flops 15040512 | bytes 7077888 | tf_op jit(solution)/shard_map/add | solution.py:90
  110.1 7.5 %fusion.29 = f32[3,24,96,128]{3,2,1,0:T(8,128)S(1)} fusion(f32[3,24,96,128]{3,2,1,0:T(8,128)S(1)} %multiply_add_fusion), kind=kLoop, calls=%fused_computation.49 | loop fusion | flops 15925248 | bytes 7077888 | tf_op jit(solution)/shard_map/mul | solution.py:159
  117.6 8.7 %fusion.137 = f32[1,3,24,96,128]{4,3,2,1,0:T(8,128)} fusion(f32[3,24,96,128]{3,2,1,0:T(8,128)S(1)} %multiply_add_fusion), kind=kLoop, calls=%fused_computation.235 | loop fusion | flops 15925248 | bytes 7077888 | tf_op jit(solution)/shard_map/broadcast_in_dim | solution.py:161
  126.3 0.0 copy-start.1
  126.3 3.1 %fusion.120 = f32[1,24,96,128]{3,2,1,0:T(8,128)} fusion(f32[24,96,128]{2,1,0:T(8,128)S(1)} %bitcast.110, f32[1,96,128]{2,1,0:T(8,128)} %collective-permute-done.1, f32[1,96,128]{2,1,0:T(8,128)} %collective-permute-done, f32[3,24,96,128]{3,2,1,0:T(8,128)S(1)} %fusion.29), kind=kLoop, calls=%fused_computation.198 | loop fusion | flops 7667712 | bytes 5996544 | tf_op jit(solution)/shard_map/broadcast_in_dim | solution.py:161
  129.3 0.0 copy-done.1
  (4 shorter events, 0.1 us)
Async XLA Ops:
  7.2 6.9 %copy-start = (s32[3,2]{0,1:T(2,128)S(1)}, s32[3,2]{0,1:T(2,128)}, u32[]{:S(2)}) copy-start(s32[3,2]{0,1:T(2,128)} %param.3) | copy-start | bytes 76
  7.2 1.3 copy-start.2
  7.2 39.6 %all-gather.2.cloned.1.call-start = ((), (), s32[]{:S(2)}) async-start(), calls=%async_computation | async-start | bytes 3538944 | tf_op jit(solution)/shard_map/all_gather | solution.py:140
  8.5 51.9 %collective-permute-start = (f32[1,96,128]{2,1,0:T(8,128)S(1)}, f32[1,96,128]{2,1,0:T(8,128)}, u32[]{:S(2)}, u32[]{:S(2)}) collective-permute-start(f32[1,96,128]{2,1,0:T(8,128)S(1)} %get-tuple-element.24), channel_id=1, source_target_pairs={{0,1},{1,2},{2,3},{3,4},{4,5},{5,6},{6,7},{7,8},{8,9},{9,10},{10,1... | collective-permute-start | bytes 147464 | tf_op jit(solution)/shard_map/ppermute | solution.py:25
  12.2 48.2 %collective-permute-start.1 = (f32[1,96,128]{2,1,0:T(8,128)S(1)}, f32[1,96,128]{2,1,0:T(8,128)}, u32[]{:S(2)}, u32[]{:S(2)}) collective-permute-start(f32[1,96,128]{2,1,0:T(8,128)S(1)} %get-tuple-element.25), channel_id=1, source_target_pairs={{1,0},{2,1},{3,2},{4,3},{5,4},{6,5},{7,6},{8,7},{9,8},{10,9},{11,1... | collective-permute-start | bytes 147464 | tf_op jit(solution)/shard_map/ppermute | solution.py:26
  56.7 9.9 %collective-permute-start.2 = (f32[3,1,96,128]{3,2,1,0:T(8,128)S(1)}, f32[3,1,96,128]{3,2,1,0:T(8,128)S(1)}, u32[]{:S(2)}, u32[]{:S(2)}) collective-permute-start(f32[3,1,96,128]{3,2,1,0:T(8,128)S(1)} %get-tuple-element.18), channel_id=1, source_target_pairs={{0,1},{1,2},{2,3},{3,4},{4,5},{5,6},{6,7},{7,8},{8,9},{9,10},{10,1... | collective-permute-start | bytes 442376 | tf_op jit(solution)/shard_map/ppermute | solution.py:25
  64.4 6.5 %collective-permute-start.3 = (f32[3,1,96,128]{3,2,1,0:T(8,128)S(1)}, f32[3,1,96,128]{3,2,1,0:T(8,128)S(1)}, u32[]{:S(2)}, u32[]{:S(2)}) collective-permute-start(f32[3,1,96,128]{3,2,1,0:T(8,128)S(1)} %get-tuple-element.17), channel_id=1, source_target_pairs={{1,0},{2,1},{3,2},{4,3},{5,4},{6,5},{7,6},{8,7},{9,8},{10,9},{11,1... | collective-permute-start | bytes 442376 | tf_op jit(solution)/shard_map/ppermute | solution.py:26
  76.9 6.6 %copy-start.3 = (f32[1,24,96,128]{3,2,1,0:T(8,128)S(1)}, f32[1,24,96,128]{3,2,1,0:T(8,128)}, u32[]{:S(2)}) copy-start(f32[1,24,96,128]{3,2,1,0:T(8,128)} %get-tuple-element.23) | copy-start | bytes 3538948
  84.1 15.6 %collective-permute-start.4 = (f32[3,4,96,128]{3,2,1,0:T(8,128)S(1)}, f32[3,4,96,128]{3,2,1,0:T(8,128)S(1)}, u32[]{:S(2)}, u32[]{:S(2)}) collective-permute-start(f32[3,4,96,128]{3,2,1,0:T(8,128)S(1)} %get-tuple-element.13), channel_id=1, source_target_pairs={{0,1},{1,2},{2,3},{3,4},{4,5},{5,6},{6,7},{7,8},{8,9},{9,10},{10,1... | collective-permute-start | bytes 1769480 | tf_op jit(solution)/shard_map/ppermute | solution.py:25
  86.5 15.6 %collective-permute-start.5 = (f32[3,4,96,128]{3,2,1,0:T(8,128)S(1)}, f32[3,4,96,128]{3,2,1,0:T(8,128)S(1)}, u32[]{:S(2)}, u32[]{:S(2)}) collective-permute-start(f32[3,4,96,128]{3,2,1,0:T(8,128)S(1)} %get-tuple-element.14), channel_id=1, source_target_pairs={{1,0},{2,1},{3,2},{4,3},{5,4},{6,5},{7,6},{8,7},{9,8},{10,9},{11,1... | collective-permute-start | bytes 1769480 | tf_op jit(solution)/shard_map/ppermute | solution.py:26
  126.3 3.1 %copy-start.1 = (s32[3,2]{0,1:T(2,128)S(1)}, s32[3,2]{0,1:T(2,128)}, u32[]{:S(2)}) copy-start(s32[3,2]{0,1:T(2,128)} %param.3) | copy-start | bytes 76
Sparse Core Ops, SparseCore 0:
  9.6 37.2 all-gather.1
where the time goes:
time: 137 us; the launch traced here: 136 us
  waiting for transfers between devices  48.1 us (35%)
  other arithmetic  42.9 us (31%)
  starting transfers between devices  16 us (12%)
  between operations  14.3 us (10%)
  matrix products  8.83 us (6%)
  local copies, waits for them, and re-layouts  6.05 us (4%)
    all_gather x1, waiting for transfers between devices, fetch_partners(): piece_block = lax.all_gather(stacked, 'img', axis=0, tiled=True)  32.7 us
    broadcast_in_dim x2, other arithmetic, shards(): return (advected[None], velocity[None])  11.7 us
    ppermute x3, waiting for transfers between devices, extended_2(): before = lax.ppermute(last, axis, up)  11 us
    ppermute x3, starting transfers between devices, extended_2(): before = lax.ppermute(last, axis, up)  9.79 us
    dot_general x1, matrix products, fetch_partners(): jnp.einsum('kn,nryz->kryz', selector, piece_block, precision=lax.Precisio...  8.83 us
    mul x1, other arithmetic, shards(): velocity = step_scale * smoothed  7.53 us
    add x6, other arithmetic, sum_three_valid(): window(volume, dimension, 0, length) + window(volume, dimension, 1, length)  6.9 us
    add x1, other arithmetic, drive_total(): drive_sum = pair_term if drive_sum is None else drive_sum + pair_term  6.62 us
  transfers between devices with their start and end apart: 7, of which 4 were waited for; matrix products, arithmetic and copies ran while one was open for 13% of the time, Pallas kernels for 0%

commit v1 on v0

v1 whole, which is shorter than its diff:
```python
import functools
import math

import jax
import jax.numpy as jnp
from jax import lax
from jax.experimental import pallas as pl
from jax.experimental.pallas import tpu as pltpu
from jax.sharding import PartitionSpec as P

RADIUS = 4
PAIRINGS = 3
HALO = RADIUS + 1
TILE = 8

gauss_sigma = 1.5
step_scale = 8.0
floor_product = 0.25
floor_variance = 0.5

CUTS = (0, 12)


def gauss_taps(radius):
    raw_taps = [
        math.exp(-(offset * offset) / (2.0 * gauss_sigma * gauss_sigma))
        for offset in range(-radius, radius + 1)
    ]
    total_weight = sum(raw_taps)
    return [raw_weight / total_weight for raw_weight in raw_taps]


WEIGHTS = gauss_taps(RADIUS)


def convolve(values, weights):
    half = len(weights) // 2
    result = weights[half] * values[half]
    for t in range(1, half + 1):
        result = result + weights[half + t] * (values[half - t] + values[half + t])
    return result


def band_matrix(width):
    row = lax.broadcasted_iota(jnp.int32, (width, width), 0)
    column = lax.broadcasted_iota(jnp.int32, (width, width), 1)
    away = jnp.abs(row - column)
    band = jnp.zeros((width, width), jnp.float32)
    for t in range(RADIUS + 1):
        band = jnp.where(away == t, WEIGHTS[RADIUS + t], band)
    high = band.astype(jnp.bfloat16)
    low = (band - high.astype(jnp.float32)).astype(jnp.bfloat16)
    above = jnp.concatenate([high, low], axis=1)
    below = jnp.concatenate([high, jnp.zeros_like(low)], axis=1)
    return jnp.concatenate([above, below], axis=0)


class Strip:
    def __init__(self, first, last, tiles, rows, width, partners):
        self.first, self.last, self.tiles = first, last, tiles
        self.rows, self.width, self.partners = rows, width, partners
        self.count = last - first
        self.low = max(first - 1, 0)
        self.high = min(last + 1, tiles)
        self.at_low, self.at_high = first == 0, last == tiles

    def local(self, tile):
        return tile - self.first + 1


def strip_kernel(strip, cuts, aliased, *refs):
    rows, width, partners = strip.rows, strip.width, strip.partners
    count = strip.count
    pieces = len(cuts)
    scalars, image, own_up, own_down, edge, far_up, far_down = refs[:7]
    middles = refs[7 : 7 + pieces]
    refs = refs[7 + pieces :]
    if aliased:
        refs = refs[2:]
    advected_out, velocity_out, a_buf, b_buf, d_buf, f_buf, v_buf, o_buf, in_sem, out_sem = refs

    def place(tile):
        return TILE * (strip.local(tile) + 1)

    span = TILE * (strip.high - strip.low)
    source = pl.ds(TILE * strip.low, span)
    target = pl.ds(place(strip.low), span)
    copies = []

    def fetch(src, dst):
        copy = pltpu.make_async_copy(src, dst, in_sem)
        copy.start()
        copies.append(copy)

    fetch(image.at[0, :, source, :], a_buf.at[pl.ds(HALO, rows), target, :])
    fetch(own_up.at[:, source, :], a_buf.at[pl.ds(0, HALO), target, :])
    fetch(own_down.at[:, source, :], a_buf.at[pl.ds(HALO + rows, HALO), target, :])
    for k in range(partners):
        fetch(edge.at[k, pl.ds(0, HALO), source, :], b_buf.at[k, pl.ds(HALO, HALO), target, :])
        fetch(edge.at[k, pl.ds(HALO, HALO), source, :], b_buf.at[k, pl.ds(rows, HALO), target, :])
        fetch(far_up.at[k, :, source, :], b_buf.at[k, pl.ds(0, HALO), target, :])
        fetch(far_down.at[k, :, source, :], b_buf.at[k, pl.ds(HALO + rows, HALO), target, :])
        for (begin, end), middle in zip(cuts, middles):
            low, high = max(begin, strip.low), min(end, strip.high)
            size = TILE * (high - low)
            fetch(
                middle.at[k, :, pl.ds(TILE * (low - begin), size), :],
                b_buf.at[k, pl.ds(2 * HALO, rows - 2 * HALO), pl.ds(place(low), size), :],
            )

    zero_tile = jnp.zeros((TILE, width), jnp.float32)
    for edge_here, tile in ((strip.at_low, 0), (strip.at_high, count + 1)):
        if edge_here:
            for i in range(rows + 2 * HALO):
                a_buf[i, pl.ds(TILE * (tile + 1), TILE), :] = zero_tile
                for k in range(partners):
                    b_buf[k, i, pl.ds(TILE * (tile + 1), TILE), :] = zero_tile
            for c in range(3):
                for r in range(rows):
                    f_buf[c, r, pl.ds(TILE * tile, TILE), :] = zero_tile

    bands = band_matrix(width)
    lane = lax.broadcasted_iota(jnp.int32, (TILE, width), 1)
    first_lane, last_lane = lane == 0, lane == width - 1

    def z_before(v):
        return jnp.where(first_lane, 0.0, pltpu.roll(v, 1, 1))

    def z_after(v):
        return jnp.where(last_lane, 0.0, pltpu.roll(v, width - 1, 1))

    for copy in copies:
        copy.wait()

    begin_tile = 1 if strip.at_low else 0
    end_tile = count + 1 if strip.at_high else count + 2
    drive_rows = rows + 2 * RADIUS
    ninth = 1.0 / 9.0

    self_weight = scalars[2]
    pair_weights = [scalars[3 + k] for k in range(partners)]

    def drive_tile(tile, carry):
        base = TILE * (tile + 1)

        def y_sums(i):
            def around(ref, *index):
                return [ref[(*index, pl.ds(base + s, TILE), slice(None))] for s in (-1, 0, 1)]

            def total(parts):
                return parts[0] + parts[1] + parts[2]

            a = around(a_buf, i)
            sums = [total(a), total([v * v for v in a])]
            centers = [a[1]]
            for k in range(partners):
                b = around(b_buf, k, i)
                sums += [total(b), total([v * v for v in b]), total([p * q for p, q in zip(a, b)])]
                centers.append(b[1])
            return sums, centers

        def finish(j, sums, centers):
            valid = scalars[0] if j < RADIUS else scalars[1] if j >= RADIUS + rows else None
            a = centers[0]
            mean_a = sums[0] * ninth
            spread_a = sums[1] * ninth - mean_a * mean_a
            guarded = jnp.maximum(spread_a, floor_variance)
            center_a = a - mean_a
            own = (2.0 * self_weight / floor_product) * spread_a
            own = own * jnp.maximum(1.0 - spread_a * (1.0 / floor_variance), 0.0)
            result = own * center_a
            for k in range(partners):
                sum_b, sum_bb, sum_ab = sums[2 + 3 * k : 5 + 3 * k]
                mean_b = sum_b * ninth
                cross = sum_ab * ninth - mean_a * mean_b
                spread_b = sum_bb * ninth - mean_b * mean_b
                product = jnp.maximum(spread_a * spread_b, floor_product)
                rest = (centers[1 + k] - mean_b) * guarded - cross * center_a
                result = result + (2.0 * pair_weights[k]) * cross * rest / (product * guarded)
            if valid is not None:
                result = result * valid
            d_buf[j, pl.ds(pl.multiple_of(TILE * tile, TILE), TILE), :] = result

        window = [y_sums(0), y_sums(1)]
        for j in range(0, drive_rows, 2):
            window += [y_sums(j + 2), y_sums(j + 3)]
            shared = [p + q for p, q in zip(window[1][0], window[2][0])]
            finish(j, [p + q for p, q in zip(window[0][0], shared)], window[1][1])
            finish(j + 1, [p + q for p, q in zip(shared, window[3][0])], window[2][1])
            window = window[2:]
        return carry

    lax.fori_loop(begin_tile, end_tile, drive_tile, 0)

    scaled = [w * (0.5 * step_scale) for w in WEIGHTS]

    def force_tile(tile, carry):
        base = TILE * (tile + 1)
        here = pl.ds(pl.multiple_of(TILE * tile, TILE), TILE)
        forces = ([], [], [])
        for j in range(drive_rows):
            drive = d_buf[j, here, :]
            a = a_buf[j + 1, pl.ds(base, TILE), :]
            forces[0].append(
                drive * (a_buf[j + 2, pl.ds(base, TILE), :] - a_buf[j, pl.ds(base, TILE), :])
            )
            forces[1].append(
                drive
                * (a_buf[j + 1, pl.ds(base + 1, TILE), :] - a_buf[j + 1, pl.ds(base - 1, TILE), :])
            )
            forces[2].append(drive * (z_after(a) - z_before(a)))
            r = j - 2 * RADIUS
            if r >= 0:
                for c in range(3):
                    f_buf[c, r, here, :] = convolve(forces[c][r : r + 2 * RADIUS + 1], scaled)
        return carry

    lax.fori_loop(begin_tile, end_tile, force_tile, 0)

    def finish_row(r, carry):
        smooth = []
        for c in range(3):
            for tile in range(1, count + 1):
                taps = [
                    f_buf[c, r, pl.ds(TILE * tile + s, TILE), :] for s in range(-RADIUS, RADIUS + 1)
                ]
                smooth.append(convolve(taps, WEIGHTS))
        smooth = jnp.concatenate(smooth, axis=0)
        high = smooth.astype(jnp.bfloat16)
        low = (smooth - high.astype(jnp.float32)).astype(jnp.bfloat16)
        both = jnp.dot(
            jnp.concatenate([high, low], axis=1), bands, preferred_element_type=jnp.float32
        )
        velocity = both[:, :width] + both[:, width:]
        for tile in range(1, count + 1):
            base = TILE * (tile + 1)
            i = r + HALO
            a = a_buf[i, pl.ds(base, TILE), :]
            neighbours = (
                (a_buf[i - 1, pl.ds(base, TILE), :], a_buf[i + 1, pl.ds(base, TILE), :]),
                (a_buf[i, pl.ds(base - 1, TILE), :], a_buf[i, pl.ds(base + 1, TILE), :]),
                (z_before(a), z_after(a)),
            )
            change = None
            there = pl.ds(TILE * (tile - 1), TILE)
            for c, (before, after) in enumerate(neighbours):
                at = TILE * (count * c + tile - 1)
                v = velocity[at : at + TILE]
                v_buf[c, r, there, :] = v
                part = v * jnp.where(v > 0.0, a - before, after - a)
                change = part if change is None else change + part
            o_buf[r, there, :] = a - change
        return carry

    there = pl.ds(TILE * strip.first, TILE * count)
    groups = 3
    each = rows // groups
    copies = []
    for g in range(groups):
        lax.fori_loop(g * each, (g + 1) * each, finish_row, 0)
        some = pl.ds(g * each, each)
        for src, dst in (
            (o_buf.at[some], advected_out.at[0, some, there, :]),
            (v_buf.at[:, some], velocity_out.at[0, :, some, there, :]),
        ):
            copy = pltpu.make_async_copy(src, dst, out_sem)
            copy.start()
            copies.append(copy)
    for copy in copies:
        copy.wait()


def run_strip(first, last, scalars, images, own_halos, edge, far_halos, middles, cuts, previous):
    _, rows, height, width = images.shape
    partners = edge.shape[0]
    strip = Strip(first, last, height // TILE, rows, width, partners)
    used = [
        (cut, middle)
        for cut, middle in zip(cuts, middles)
        if cut[0] < strip.high and cut[1] > strip.low
    ]
    operands = [scalars, images, *own_halos, edge, *far_halos, *(m for _, m in used)]
    in_specs = [pl.BlockSpec(memory_space=pltpu.SMEM)]
    in_specs += [pl.BlockSpec(memory_space=pl.ANY)] * (len(operands) - 1)
    aliases = {}
    if previous is not None:
        aliases = {len(operands): 0, len(operands) + 1: 1}
        operands += list(previous)
        in_specs += [pl.BlockSpec(memory_space=pl.ANY)] * 2
    extended, count = rows + 2 * HALO, strip.count
    f32 = jnp.float32
    voxels = rows * count * TILE * width
    return pl.pallas_call(
        functools.partial(
            strip_kernel, strip, [cut for cut, _ in used], previous is not None
        ),
        out_shape=(
            jax.ShapeDtypeStruct((1, rows, height, width), f32),
            jax.ShapeDtypeStruct((1, 3, rows, height, width), f32),
        ),
        in_specs=in_specs,
        out_specs=(pl.BlockSpec(memory_space=pl.ANY),) * 2,
        scratch_shapes=[
            pltpu.VMEM((extended, TILE * (count + 4), width), f32),
            pltpu.VMEM((partners, extended, TILE * (count + 4), width), f32),
            pltpu.VMEM((rows + 2 * RADIUS, TILE * (count + 2), width), f32),
            pltpu.VMEM((3, rows, TILE * (count + 2), width), f32),
            pltpu.VMEM((3, rows, TILE * count, width), f32),
            pltpu.VMEM((rows, TILE * count, width), f32),
            pltpu.SemaphoreType.DMA,
            pltpu.SemaphoreType.DMA,
        ],
        input_output_aliases=aliases,
        compiler_params=pltpu.CompilerParams(vmem_limit_bytes=40 * 2**20),
        cost_estimate=pl.CostEstimate(
            flops=250 * voxels, bytes_accessed=24 * voxels, transcendentals=0
        ),
        name=f"strip_{first}_{last}",
    )(*operands)


def shards(images, pairings):
    peers = lax.axis_size("img")
    slabs = lax.axis_size("space")
    me = lax.axis_index("img")
    slab = lax.axis_index("space")
    _, rows, height, width = images.shape
    partner_ids = lax.dynamic_slice_in_dim(pairings, me, 1, 1)[:, 0]
    up = [(i, i + 1) for i in range(slabs - 1)]
    down = [(i + 1, i) for i in range(slabs - 1)]

    if peers == 2:
        self_weight = jnp.sum((partner_ids == me).astype(jnp.float32))
        weights = [PAIRINGS - self_weight]

        def partners_of(piece):
            return lax.ppermute(piece, "img", [(0, 1), (1, 0)])

    else:
        self_weight = jnp.float32(0.0)
        weights = [jnp.float32(1.0)] * PAIRINGS

        def partners_of(piece):
            every = lax.all_gather(piece, "img", axis=0, tiled=True)
            return jnp.concatenate(
                [lax.dynamic_slice_in_dim(every, partner_ids[k], 1, 0) for k in range(PAIRINGS)]
            )

    scalars = jnp.stack(
        [(slab > 0).astype(jnp.float32), (slab < slabs - 1).astype(jnp.float32), self_weight, *weights]
    )

    own = images[0]
    edge = partners_of(jnp.concatenate([images[:, :HALO], images[:, rows - HALO :]], axis=1))
    cuts = list(zip(CUTS[:-1], CUTS[1:]))
    middles = [
        partners_of(images[:, HALO : rows - HALO, TILE * low : TILE * high]) for low, high in cuts
    ]
    own_halos = (
        lax.ppermute(own[rows - HALO :], "space", up),
        lax.ppermute(own[:HALO], "space", down),
    )
    far_halos = (
        lax.ppermute(edge[:, HALO:], "space", up),
        lax.ppermute(edge[:, :HALO], "space", down),
    )
    tiles = height // TILE
    ends = [high - 1 if high < tiles else tiles for _, high in cuts]
    first, outputs = 0, None
    for last in ends:
        outputs = run_strip(
            first, last, scalars, images, own_halos, edge, far_halos, middles, cuts, outputs
        )
        first = last
    return outputs


def solution(mesh):
    return jax.shard_map(
        shards,
        mesh=mesh,
        in_specs=(P("img", "space", None, None), P()),
        out_specs=(P("img", "space", None, None), P("img", None, "space", None, None)),
        check_vma=False,
    )
```

time: 137 us -> 44.9 us (0.33)
  the two profiles are of different devices: /device:TPU:9 before, /device:TPU:0 now
where the time goes in v1:
time: 44.9 us; the launch traced here: 44.7 us
  waiting for transfers between devices  15.1 us (34%)
  Pallas kernels  13 us (29%)
  starting transfers between devices  10.1 us (22%)
  local copies, waits for them, and re-layouts  3.72 us (8%)
  other arithmetic  1.39 us (3%)
  between operations  1.33 us (3%)
    ppermute x2, waiting for transfers between devices, partners_of(): return lax.ppermute(piece, 'img', [(0, 1), (1, 0)])  15.1 us
    pallas_call x1, Pallas kernels, run_strip(): pl.pallas_call(functools.partial(strip_kernel, strip, [cut for cut, _ in...  13 us
    ppermute x2, starting transfers between devices, partners_of(): return lax.ppermute(piece, 'img', [(0, 1), (1, 0)])  3.05 us
    ppermute x1, starting transfers between devices, shards(): lax.ppermute(edge[:, HALO:], 'space', up)  3.04 us
    slice x1, local copies, waits for them, and re-layouts, shards(): own[:HALO]  2 us
    ppermute x1, starting transfers between devices, shards(): lax.ppermute(own[rows - HALO:], 'space', up)  1.46 us
    ppermute x1, starting transfers between devices, shards(): lax.ppermute(own[:HALO], 'space', down)  1.29 us
    ppermute x1, starting transfers between devices, shards(): lax.ppermute(edge[:, :HALO], 'space', down)  1.28 us
  transfers between devices with their start and end apart: 6, of which 2 were waited for; matrix products, arithmetic and copies ran while one was open for 7% of the time, Pallas kernels for 0%

profile of v1, /device:TPU:0, one launch (start us, length us, event | category | flops | bytes accessed | tf_op | source)
XLA Modules:
  0.0 44.7 jit_solution(3555233471284066110)
XLA Ops:
  0.6 0.0 copy-start
  0.6 2.0 %fusion.1 = (f32[1,5,96,128]{3,2,1,0:T(8,128)S(1)}, f32[5,96,128]{2,1,0:T(8,128)}, f32[5,96,128]{2,1,0:T(8,128)}, f32[1,5,96,128]{3,2,1,0:T(8,128)S(1)}) fusion(f32[1,24,96,128]{3,2,1,0:T(8,128)} %refs_1_.1), kind=kLoop, calls=%fused_computation.6 | loop fusion | bytes 1474560 | tf_op jit(solution)/shard_map/slice | solution.py:361
  2.7 0.0 copy-start.1
  2.7 3.0 %collective-permute-start.2 = (f32[1,10,96,128]{3,2,1,0:T(8,128)S(1)}, f32[1,10,96,128]{3,2,1,0:T(8,128)S(1)}, u32[]{:S(2)}, u32[]{:S(2)}) collective-permute-start(f32[1,10,96,128]{3,2,1,0:T(8,128)S(1)} %pad_maximum_fusion), channel_id=1, source_target_pairs={{0,16},{16,0},{1,17},{17,1},{2,18},{18,2},{3,19},{19,3},{4,20},{20... | collective-permute-start | bytes 1474568 | tf_op jit(solution)/shard_map/ppermute | solution.py:337
  5.7 0.0 copy-done
  5.7 0.9 %slice.29 = f32[1,14,96,128]{3,2,1,0:T(8,128)} slice(f32[1,24,96,128]{3,2,1,0:T(8,128)S(1)} %copy-done), slice={[0:1], [5:19], [0:96], [0:128]} | slice | bytes 1376256 | tf_op jit(solution)/shard_map/slice | solution.py:357
  6.6 0.0 collective-permute-start.5
  6.6 1.5 %collective-permute-start = (f32[5,96,128]{2,1,0:T(8,128)}, f32[5,96,128]{2,1,0:T(8,128)S(1)}, u32[]{:S(2)}, u32[]{:S(2)}) collective-permute-start(f32[5,96,128]{2,1,0:T(8,128)} %get-tuple-element.3), channel_id=1, source_target_pairs={{0,1},{1,2},{2,3},{3,4},{4,5},{5,6},{6,7},{7,8},{8,9},{9,10},{10,1... | collective-permute-start | bytes 737288 | tf_op jit(solution)/shard_map/ppermute | solution.py:360
  8.1 1.3 %collective-permute-start.1 = (f32[5,96,128]{2,1,0:T(8,128)}, f32[5,96,128]{2,1,0:T(8,128)S(1)}, u32[]{:S(2)}, u32[]{:S(2)}) collective-permute-start(f32[5,96,128]{2,1,0:T(8,128)} %get-tuple-element.4), channel_id=1, source_target_pairs={{1,0},{2,1},{3,2},{4,3},{5,4},{6,5},{7,6},{8,7},{9,8},{10,9},{11,1... | collective-permute-start | bytes 737288 | tf_op jit(solution)/shard_map/ppermute | solution.py:361
  9.4 8.4 %collective-permute-done.2.refs_4_ = f32[1,10,96,128]{3,2,1,0:T(8,128)S(1)} collective-permute-done((f32[1,10,96,128]{3,2,1,0:T(8,128)S(1)}, f32[1,10,96,128]{3,2,1,0:T(8,128)S(1)}, u32[]{:S(2)}, u32[]{:S(2)}) %collective-permute-start.2) | collective-permute-done | bytes 491552 | tf_op jit(solution)/shard_map/ppermute | solution.py:337
  17.8 0.8 %fusion.2 = (f32[1,5,96,128]{3,2,1,0:T(8,128)}, f32[1,5,96,128]{3,2,1,0:T(8,128)}) fusion(f32[1,10,96,128]{3,2,1,0:T(8,128)S(1)} %collective-permute-done.2.refs_4_), kind=kLoop, calls=%fused_computation.7 | loop fusion | bytes 983040 | tf_op jit(solution)/shard_map/slice | solution.py:365
  18.6 1.3 %collective-permute-start.4 = (f32[1,5,96,128]{3,2,1,0:T(8,128)}, f32[1,5,96,128]{3,2,1,0:T(8,128)S(1)}, u32[]{:S(2)}, u32[]{:S(2)}) collective-permute-start(f32[1,5,96,128]{3,2,1,0:T(8,128)} %get-tuple-element.6), channel_id=1, source_target_pairs={{1,0},{2,1},{3,2},{4,3},{5,4},{6,5},{7,6},{8,7},{9,8},{10,9},{11,1... | collective-permute-start | bytes 737288 | tf_op jit(solution)/shard_map/ppermute | solution.py:365
  19.9 3.0 %collective-permute-start.3 = (f32[1,5,96,128]{3,2,1,0:T(8,128)}, f32[1,5,96,128]{3,2,1,0:T(8,128)S(1)}, u32[]{:S(2)}, u32[]{:S(2)}) collective-permute-start(f32[1,5,96,128]{3,2,1,0:T(8,128)} %get-tuple-element.7), channel_id=1, source_target_pairs={{0,1},{1,2},{2,3},{3,4},{4,5},{5,6},{6,7},{7,8},{8,9},{9,10},{10,1... | collective-permute-start | bytes 737288 | tf_op jit(solution)/shard_map/ppermute | solution.py:364
  22.9 0.0 copy-done.1
  23.0 0.7 %fusion = f32[]{:T(128)} fusion(s32[3,2]{0,1:T(2,128)S(1)} %copy-done.1, s32[]{:T(128)S(6)} %select_n.3, s32[]{:T(128)S(6)} %axis_index.25), kind=kLoop, calls=%fused_computation.2 | loop fusion | flops 8 | bytes 24 | tf_op jit(solution)/shard_map/reduce_sum | solution.py:333
  24.2 0.7 %pad_maximum_fusion.1.refs_0_ = f32[4]{0:T(128)S(1)} fusion(f32[1]{0:T(128)} %bitcast.3, f32[1]{0:T(128)} %bitcast.2, f32[1]{0:T(128)} %bitcast.1, f32[1]{0:T(128)} %bitcast), kind=kLoop, calls=%fused_computation.3 | loop fusion | flops 12 | bytes 32 | tf_op jit(solution)/shard_map/stack | solution.py:349
  24.9 0.0 collective-permute-done.refs_2_
  24.9 0.0 collective-permute-done.1.refs_3_
  24.9 6.7 %collective-permute-done.5.refs_7_ = f32[1,14,96,128]{3,2,1,0:T(8,128)S(1)} collective-permute-done((f32[1,14,96,128]{3,2,1,0:T(8,128)}, f32[1,14,96,128]{3,2,1,0:T(8,128)S(1)}, u32[]{:S(2)}, u32[]{:S(2)}) %collective-permute-start.5) | collective-permute-done | bytes 688160 | tf_op jit(solution)/shard_map/ppermute | solution.py:337
  31.7 0.0 collective-permute-done.4.refs_6_
  31.7 0.0 collective-permute-done.3.refs_5_
  31.7 13.0 %strip_0_12.1 = (f32[1,24,96,128]{3,2,1,0:T(8,128)}, f32[1,3,24,96,128]{4,3,2,1,0:T(8,128)}) custom-call(f32[4]{0:T(128)S(1)} %pad_maximum_fusion.1.refs_0_, f32[1,24,96,128]{3,2,1,0:T(8,128)S(1)} %copy-done, f32[5,96,128]{2,1,0:T(8,128)S(1)} %collective-permute-done.refs_2_, f32[5,96,128]{2,1,0:T(8,128)S(1)} %collective-permute-done.1.refs_3_, ...), custom_call_target="tpu_custom_call" | custom-call | flops 73728000 | bytes 7077888 | tf_op jit(solution)/shard_map/strip_0_12/pallas_call | solution.py:293
  (1 shorter events, 0.0 us)
Async XLA Ops:
  0.6 5.1 %copy-start = (f32[1,24,96,128]{3,2,1,0:T(8,128)S(1)}, f32[1,24,96,128]{3,2,1,0:T(8,128)}, u32[]{:S(2)}) copy-start(f32[1,24,96,128]{3,2,1,0:T(8,128)} %refs_1_.1) | copy-start | bytes 3538948
  2.7 20.3 %copy-start.1 = (s32[3,2]{0,1:T(2,128)S(1)}, s32[3,2]{0,1:T(2,128)}, u32[]{:S(2)}) copy-start(s32[3,2]{0,1:T(2,128)} %param.3) | copy-start | bytes 76
  2.7 15.1 %collective-permute-start.2 = (f32[1,10,96,128]{3,2,1,0:T(8,128)S(1)}, f32[1,10,96,128]{3,2,1,0:T(8,128)S(1)}, u32[]{:S(2)}, u32[]{:S(2)}) collective-permute-start(f32[1,10,96,128]{3,2,1,0:T(8,128)S(1)} %pad_maximum_fusion), channel_id=1, source_target_pairs={{0,16},{16,0},{1,17},{17,1},{2,18},{18,2},{3,19},{19,3},{4,20},{20... | collective-permute-start | bytes 1474568 | tf_op jit(solution)/shard_map/ppermute | solution.py:337
  6.6 25.1 %collective-permute-start.5 = (f32[1,14,96,128]{3,2,1,0:T(8,128)}, f32[1,14,96,128]{3,2,1,0:T(8,128)S(1)}, u32[]{:S(2)}, u32[]{:S(2)}) collective-permute-start(f32[1,14,96,128]{3,2,1,0:T(8,128)} %slice.29), channel_id=1, source_target_pairs={{0,16},{16,0},{1,17},{17,1},{2,18},{18,2},{3,19},{19,3},{4,20},{20... | collective-permute-start | bytes 2064392 | tf_op jit(solution)/shard_map/ppermute | solution.py:337
  6.6 18.3 %collective-permute-start = (f32[5,96,128]{2,1,0:T(8,128)}, f32[5,96,128]{2,1,0:T(8,128)S(1)}, u32[]{:S(2)}, u32[]{:S(2)}) collective-permute-start(f32[5,96,128]{2,1,0:T(8,128)} %get-tuple-element.3), channel_id=1, source_target_pairs={{0,1},{1,2},{2,3},{3,4},{4,5},{5,6},{6,7},{7,8},{8,9},{9,10},{10,1... | collective-permute-start | bytes 737288 | tf_op jit(solution)/shard_map/ppermute | solution.py:360
  8.1 16.8 %collective-permute-start.1 = (f32[5,96,128]{2,1,0:T(8,128)}, f32[5,96,128]{2,1,0:T(8,128)S(1)}, u32[]{:S(2)}, u32[]{:S(2)}) collective-permute-start(f32[5,96,128]{2,1,0:T(8,128)} %get-tuple-element.4), channel_id=1, source_target_pairs={{1,0},{2,1},{3,2},{4,3},{5,4},{6,5},{7,6},{8,7},{9,8},{10,9},{11,1... | collective-permute-start | bytes 737288 | tf_op jit(solution)/shard_map/ppermute | solution.py:361
  18.6 13.1 %collective-permute-start.4 = (f32[1,5,96,128]{3,2,1,0:T(8,128)}, f32[1,5,96,128]{3,2,1,0:T(8,128)S(1)}, u32[]{:S(2)}, u32[]{:S(2)}) collective-permute-start(f32[1,5,96,128]{3,2,1,0:T(8,128)} %get-tuple-element.6), channel_id=1, source_target_pairs={{1,0},{2,1},{3,2},{4,3},{5,4},{6,5},{7,6},{8,7},{9,8},{10,9},{11,1... | collective-permute-start | bytes 737288 | tf_op jit(solution)/shard_map/ppermute | solution.py:365
  19.9 11.8 %collective-permute-start.3 = (f32[1,5,96,128]{3,2,1,0:T(8,128)}, f32[1,5,96,128]{3,2,1,0:T(8,128)S(1)}, u32[]{:S(2)}, u32[]{:S(2)}) collective-permute-start(f32[1,5,96,128]{3,2,1,0:T(8,128)} %get-tuple-element.7), channel_id=1, source_target_pairs={{0,1},{1,2},{2,3},{3,4},{4,5},{5,6},{6,7},{7,8},{8,9},{9,10},{10,1... | collective-permute-start | bytes 737288 | tf_op jit(solution)/shard_map/ppermute | solution.py:364
